TPU v7x, 32 devices: a whole 2x2x4 slice. The times are simulated.
32 devices in a mesh: blk: 8 (over y, x, core), grp: 4 (over z).
Axes of the slice: x: 2, y: 2, z: 4, core: 2. Of those that a mesh axis runs over, the one named last changes fastest.
Arguments:
- queries: float32 [4096, 1024], P(('blk', 'grp')), may hold values from -48 to 48
- passages: float32 [4096, 1024], P(('blk', 'grp')), may hold values from -48 to 48
- hard_table: bfloat16 [24576, 1024], P(('blk', 'grp')), may hold values from -12 to 12
- hard_index: int32 [4096, 8], P(('blk', 'grp')), may hold values from 0 to 3071, as said below
Outputs:
- mean_loss: float32 [], replicated
- query_grad: float32 [4096, 1024], P(('blk', 'grp'))
- passage_grad: float32 [4096, 1024], P(('blk', 'grp'))
- table_grad: bfloat16 [24576, 1024], P(('blk', 'grp'))
Inputs may be any that keep to these rules, and one draw needn't show every extreme that they name: Owner o = hard_index // 768 is a batch group of the query's own loop shard. Among the 1024 entries of one device, the four owners are named exactly 384, 256, 256 and 128 times in some order, and the owner named 3 * 128 times is the same for all devices of one loop shard; entries may repeat.
All inputs are finite; a program needn't handle non-finite values.
Results may differ from a plain program's by a relative error of at most 0.0038.
Values may be sent and summed in bfloat16 or wider, within the bound.
A program may use at most 64 MiB of HBM per device.

v0:
```python
import functools

import jax
import jax.numpy as jnp
from jax import lax
from jax.experimental import pallas as pl
from jax.experimental.pallas import tpu as pltpu
from jax.sharding import PartitionSpec as P

STOPS = 4
SCALE = 0.015625
TOP = 32766.0
LOW = -1e30
MESH = pl.DeviceIdType.MESH
HIGHEST = lax.Precision.HIGHEST

QUERY, QUERY_META, PASSAGE, PASSAGE_META, STATS, PARTIAL, LSE, GRAD = range(8)


def as_column(row, count):
    return jnp.broadcast_to(row, (128, count)).T[:, 0:1]


def as_row(column, count):
    return jnp.broadcast_to(column, (count, 128)).T[0:1, :]


def coded(value):
    largest = jnp.max(jnp.abs(value), axis=1, keepdims=True)
    largest = jnp.maximum(largest, 1e-30)
    code = jnp.round(value * (TOP / largest)).astype(jnp.int32).astype(jnp.int16)
    return code, largest * (1.0 / TOP)


def halves(code):
    value = code.astype(jnp.int32).astype(jnp.float32)
    high = value.astype(jnp.bfloat16)
    return high, (value - high.astype(jnp.float32)).astype(jnp.bfloat16)


def two_terms(value):
    high = value.astype(jnp.bfloat16)
    return high, (value - high.astype(jnp.float32)).astype(jnp.bfloat16)


def mm(a, b):
    return jnp.dot(a, b, preferred_element_type=jnp.float32)


def nt(a, b, precision=None):
    return lax.dot_general(
        a, b, (((1,), (1,)), ((), ())), precision=precision, preferred_element_type=jnp.float32
    )


def kernel(
    loops, groups,
    q_hbm, p_hbm, t_hbm, idx_ref,
    loss_ref, qg_out, pg_out, tg_out,
    q_ref, p_ref, t_ref, qg_ref, pg_ref, tg_ref, q16, qmeta, p16, pmeta, st_send, st_recv, a_send, a_recv, lse_send, lse_recv,
    g_send, g_recv, l_send, l_recv, sh, ch, sw, phi, plo, gf, qhi, qlo, whi,
    send_sem, recv_sem, lsend_sem, lrecv_sem, load_sem, save_sem,
):
    b = lax.axis_index("blk")
    g = lax.axis_index("grp")
    rows, width = q_ref.shape
    table_rows = t_ref.shape[0]
    loads = [
        pltpu.make_async_copy(src, dst, load_sem.at[i])
        for i, (src, dst) in enumerate(((q_hbm, q_ref), (p_hbm, p_ref), (t_hbm, t_ref)))
    ]
    for load in loads:
        load.start()
    barrier = pltpu.get_barrier_semaphore()
    for j in range(1, groups):
        pl.semaphore_signal(
            barrier, inc=1, device_id=(b, lax.rem(g + j, groups)), device_id_type=MESH
        )

    def greet(k, carry):
        pl.semaphore_signal(
            barrier, inc=1, device_id=(lax.rem(b + k, loops), g), device_id_type=MESH
        )
        return carry

    lax.fori_loop(1, loops, greet, 0)

    def copy(kind, j, src, dst, device, slot=None):
        return pltpu.make_async_remote_copy(
            src_ref=src,
            dst_ref=dst,
            send_sem=send_sem.at[kind, j],
            recv_sem=recv_sem.at[kind, j if slot is None else slot],
            device_id=device,
            device_id_type=MESH,
        )

    copies = {}

    def go(kind, j, src, dst, device, slot=None):
        copies[kind, j] = copy(kind, j, src, dst, device, slot)
        copies[kind, j].start()

    def arrived(kind, slot, ref):
        copy(kind, 0, ref, ref, (b, lax.rem(g + 1, groups)), slot).wait_recv()

    near = jnp.minimum(g, groups - 1 - g)
    right_longer = (g < groups - 1 - g).astype(jnp.int32)
    others = [None]
    for i in range(groups - 1):
        both = (i < 2 * near).astype(jnp.int32)
        distance = both * (i // 2 + 1) + (1 - both) * (i - near + 1)
        right = both * (i % 2) + (1 - both) * right_longer
        others.append(g + distance * (2 * right - 1))

    own_right = copy(QUERY, 0, q16.at[g], q16.at[g], (b, jnp.minimum(g + 1, groups - 1)), g)
    own_left = copy(QUERY, groups, q16.at[g], q16.at[g], (b, jnp.maximum(g - 1, 0)), g)

    def onward(j):
        src = others[j]
        step = jnp.where(src < g, 1, -1)
        dst = g + step
        return (dst >= 0) & (dst < groups), copy(
            QUERY, j, q16.at[src], q16.at[src], (b, jnp.clip(dst, 0, groups - 1)), src
        )

    def receive(j):
        src = others[j]
        arrived(QUERY, src, q16.at[src])
        valid, forward = onward(j)

        @pl.when(valid)
        def _():
            forward.start()

    loads[0].wait()
    query = q_ref[...]
    code, scale = coded(query)
    q16[g] = code
    qmeta[g, 0:8, :] = idx_ref[...].astype(jnp.float32)
    qmeta[g, 8:16, :] = jnp.broadcast_to(as_row(scale, rows), (8, rows))
    pl.semaphore_wait(barrier, groups - 1 + loops - 1)

    @pl.when(g < groups - 1)
    def _():
        own_right.start()

    @pl.when(g > 0)
    def _():
        own_left.start()

    for j in range(1, groups):
        go(QUERY_META, j, qmeta.at[g], qmeta.at[g], (b, others[j]), g)
    loads[1].wait()
    code, scale = coded(p_ref[...])
    p16[0] = code
    pmeta[0] = jnp.broadcast_to(as_row(scale, rows), (8, rows))
    for s in range(1, STOPS):
        go(PASSAGE_META, s, pmeta.at[0], pmeta.at[s], (lax.rem(b + s, loops), g))
    for s in (3, 1):
        go(PASSAGE, s, p16.at[0], p16.at[s], (lax.rem(b + s, loops), g))
    loads[2].wait()

    row_id = lax.broadcasted_iota(jnp.int32, (table_rows, rows), 0).astype(jnp.float32) + (
        g * table_rows
    ).astype(jnp.float32)

    def count(j):
        src = g if j == 0 else others[j]
        named = jnp.zeros((table_rows, rows), jnp.float32)
        for k in range(8):
            named = named + jnp.where(row_id == qmeta[src, k:k + 1, :], 1.0, 0.0)
        ch[j] = named

    def hard_part(j):
        src = g if j == 0 else others[j]
        high, low = halves(q16[src])
        qhi[j * rows:(j + 1) * rows, :] = high
        qlo[j * rows:(j + 1) * rows, :] = low
        table = t_ref[...]
        both = nt(table, jnp.concatenate([high, low], axis=0))
        scores = (both[:, 0:rows] + both[:, rows:]) * (qmeta[src, 8:9, :] * SCALE)
        named = ch[j]
        top = jnp.max(jnp.where(named > 0.0, scores, LOW), axis=0, keepdims=True)
        part = named * jnp.exp(jnp.minimum(scores - top, 0.0))
        sh[j] = scores
        st_send[j, 0:1, :] = top
        st_send[j, 1:2, :] = jnp.sum(part, axis=0, keepdims=True)
        if j > 0:
            go(STATS, j, st_send.at[j], st_recv.at[g], (b, src), g)
        a_send[j] = mm(part.T.astype(jnp.bfloat16), table).astype(jnp.bfloat16)
        if j > 0:
            go(PARTIAL, j, a_send.at[j], a_recv.at[g], (b, src), g)

    def window_part(s):
        if s == 0:
            sw[0:rows, :] = nt(p_ref[...], query, HIGHEST) * SCALE
            return
        high, low = halves(p16[s])
        at = slice((s - 1) * rows, s * rows)
        phi[at, :] = high
        plo[at, :] = low
        own_high, own_low = qhi[0:rows, :], qlo[0:rows, :]
        both = nt(high, jnp.concatenate([own_high, own_low], axis=0))
        scores = both[:, 0:rows] + both[:, rows:] + nt(low, own_high)
        sw[s * rows:(s + 1) * rows, :] = (
            scores * as_column(pmeta[s, 0:1, :], rows) * (qmeta[g, 8:9, :] * SCALE)
        )

    st_send[...] = jnp.zeros_like(st_send)
    count(0)
    hard_part(0)
    window_part(0)
    for j in range(1, groups):
        arrived(QUERY_META, others[j], qmeta.at[others[j]])
        count(j)
    positive = jnp.sum(query * p_ref[...]) * SCALE
    def window_next(s):
        copies[PASSAGE_META, s].wait_recv()
        if s == 2:
            copies[PASSAGE, s].wait_recv()
        window_part(s)

    receive(1)
    if groups > 2:

        @pl.when(near > 0)
        def _():
            receive(2)

    hard_part(1)
    if groups > 2:

        @pl.when(near == 0)
        def _():
            receive(2)

    odd = lax.rem(b, 2)
    partner = b + 1 - 2 * odd
    for s in (1, 3):
        copies[PASSAGE, s].wait_recv()
    go(PASSAGE, 2, p16.at[1 + 2 * odd], p16.at[2], (partner, g))
    window_next(1)
    for j in range(2, groups):
        if j > 2:
            receive(j)
        if j == groups - 1:
            for s in range(2, STOPS):
                window_next(s)
        hard_part(j)

    window = sw[...]
    tops = [jnp.max(window, axis=0, keepdims=True), st_send[0, 0:1, :]]
    for j in range(1, groups):
        arrived(STATS, others[j], st_recv.at[others[j]])
        tops.append(st_recv[others[j], 0:1, :])
    top = functools.reduce(jnp.maximum, tops)
    total = jnp.sum(jnp.exp(window - top), axis=0, keepdims=True)
    total = total + st_send[0, 1:2, :] * jnp.exp(tops[1] - top)
    for j in range(1, groups):
        total = total + st_recv[others[j], 1:2, :] * jnp.exp(tops[j + 1] - top)
    lse = top + jnp.log(total)
    lse_send[0:1, :] = lse
    lse_send[1:8, :] = jnp.broadcast_to(jnp.sum(lse) - positive, (7, rows))
    for j in range(1, groups):
        go(LSE, j, lse_send, lse_recv.at[g], (b, others[j]), g)

    sw[...] = jnp.exp(window - lse)
    whi_, wlo_ = two_terms(sw[rows:, :] * qmeta[g, 8:9, :])
    terms = mm(
        jnp.concatenate([whi_, whi_], axis=1),
        jnp.concatenate([qhi[0:rows, :], qlo[0:rows, :]], axis=0),
    ) + mm(wlo_, qhi[0:rows, :])
    alone, joined = 3 - 2 * odd, 1 + 2 * odd
    for s in range(1, STOPS):
        term = terms[(s - 1) * rows:s * rows, :]
        gf[s - 1] = term
        g_send[s - 1] = term.astype(jnp.bfloat16)
    go(GRAD, 0, g_send.at[1], g_recv.at[0], (partner, g))
    go(GRAD, 1, g_send.at[alone - 1], g_recv.at[1], (lax.rem(b + loops - alone, loops), g))
    pg_ref[...] = jnp.dot(
        sw[0:rows, :], query, precision=HIGHEST, preferred_element_type=jnp.float32
    )

    group_loss = lse_send[1:2, :]
    whi[:, 0:rows] = (
        ch[0] * jnp.exp(jnp.minimum(sh[0] - lse, 0.0)) * (qmeta[g, 8:9, :] * SCALE)
    ).astype(jnp.bfloat16)
    for j in range(1, groups):
        arrived(LSE, others[j], lse_recv.at[others[j]])
        group_loss = group_loss + lse_recv[others[j], 1:2, :]
        whi[:, j * rows:(j + 1) * rows] = jnp.where(
            ch[j] > 0.0,
            ch[j] * jnp.exp(jnp.minimum(sh[j] - lse_recv[others[j], 0:1, :], 0.0)) * (qmeta[others[j], 8:9, :] * SCALE),
            0.0,
        ).astype(jnp.bfloat16)

    l_send[...] = jnp.broadcast_to(group_loss, (8, rows))
    l_recv[0] = jnp.broadcast_to(group_loss, (8, rows))

    def loss_copy(k):
        return pltpu.make_async_remote_copy(
            src_ref=l_send,
            dst_ref=l_recv.at[k],
            send_sem=lsend_sem.at[k],
            recv_sem=lrecv_sem.at[k],
            device_id=(lax.rem(b + k, loops), g),
            device_id_type=MESH,
        )

    def loss_start(k, carry):
        loss_copy(k).start()
        return carry

    lax.fori_loop(1, loops, loss_start, 0)

    copies[GRAD, 0].wait_recv()
    g_send[STOPS - 1] = (gf[joined - 1] + g_recv[0].astype(jnp.float32)).astype(jnp.bfloat16)
    go(GRAD, 2, g_send.at[STOPS - 1], g_recv.at[2], (lax.rem(b + loops - joined, loops), g))

    tile = 256

    def table_tile(step, carry):
        cols = pl.ds(pl.multiple_of(step * tile, tile), tile)
        left = whi[...]
        tg_ref[:, cols] = (
            jnp.dot(left, qhi[:, cols], preferred_element_type=jnp.float32)
            + jnp.dot(left, qlo[:, cols], preferred_element_type=jnp.float32)
        ).astype(jnp.bfloat16)
        return carry

    lax.fori_loop(0, width // tile, table_tile, 0)
    saves = [
        pltpu.make_async_copy(src, dst, save_sem.at[i])
        for i, (src, dst) in enumerate(((tg_ref, tg_out), (qg_ref, qg_out), (pg_ref, pg_out)))
    ]
    saves[0].start()

    whi_, wlo_ = two_terms(
        jnp.concatenate(
            [
                sw[s * rows:(s + 1) * rows, :] * as_column(pmeta[s, 0:1, :], rows)
                for s in range(1, STOPS)
            ],
            axis=0,
        ).T
    )
    qg_ref[...] = (
        jnp.dot(
            sw[0:rows, :].T, p_ref[...], precision=HIGHEST, preferred_element_type=jnp.float32
        )
        - p_ref[...]
        + (mm(whi_, phi[...]) + mm(wlo_, phi[...]) + mm(whi_, plo[...]))
    )

    parts = a_send[0].astype(jnp.float32) * as_column(jnp.exp(tops[1] - lse), rows)
    for j in range(1, groups):
        arrived(PARTIAL, others[j], a_recv.at[others[j]])
        parts = parts + a_recv[others[j]].astype(jnp.float32) * as_column(jnp.exp(tops[j + 1] - lse), rows)
    qg_ref[...] = (qg_ref[...] + parts) * SCALE
    saves[1].start()
    sums = pg_ref[...]
    for s in range(1, 3):
        copies[GRAD, s].wait_recv()
        sums = sums + g_recv[s].astype(jnp.float32)
    pg_ref[...] = (sums - query) * SCALE
    saves[2].start()

    def loss_wait(k, carry):
        loss_copy(k).wait()
        return carry

    lax.fori_loop(1, loops, loss_wait, 0)
    loss_ref[0, 0] = jnp.sum(l_recv[:, 0:1, 0:1]) / (rows * loops * groups)
    for each in copies.values():
        each.wait_send()

    @pl.when(g < groups - 1)
    def _():
        own_right.wait_send()

    @pl.when(g > 0)
    def _():
        own_left.wait_send()

    for j in range(1, groups):
        valid, forward = onward(j)

        @pl.when(valid)
        def _():
            forward.wait_send()

    for save in saves:
        save.wait()


def hand_over(a_ref, b_ref, c_ref, a_out, b_out, c_out, a_here, b_here, c_here, sem_in, sem_out):
    trips = []
    for src, here, dst in ((c_ref, c_here, c_out), (a_ref, a_here, a_out), (b_ref, b_here, b_out)):
        part = src.shape[0] // 4
        for i in range(4):
            at, k = pl.ds(i * part, part), len(trips)
            trips.append((
                pltpu.make_async_copy(src.at[at], here.at[at], sem_in.at[k]),
                pltpu.make_async_copy(here.at[at], dst.at[at], sem_out.at[k]),
            ))
    for bring, _ in trips:
        bring.start()
    for bring, store in trips:
        bring.wait()
        store.start()
    for _, store in trips:
        store.wait()


def local(loops, groups, queries, passages, hard_table, hard_index):
    rows, width = queries.shape
    table_rows = hard_table.shape[0]
    index = hard_index.T
    anywhere = pl.BlockSpec(memory_space=pl.ANY)
    vmem = pl.BlockSpec(memory_space=pltpu.VMEM)
    f32, bf16, i16 = jnp.float32, jnp.bfloat16, jnp.int16
    out = pl.pallas_call(
        functools.partial(kernel, loops, groups),
        out_shape=(
            jax.ShapeDtypeStruct((1, 1), f32),
            jax.ShapeDtypeStruct((rows, width), f32),
            jax.ShapeDtypeStruct((rows, width), f32),
            jax.ShapeDtypeStruct((table_rows, width), bf16),
        ),
        in_specs=[anywhere] * 3 + [vmem],
        out_specs=(pl.BlockSpec(memory_space=pltpu.SMEM),) + (anywhere,) * 3,
        scratch_shapes=[
            pltpu.VMEM((rows, width), f32),
            pltpu.VMEM((rows, width), f32),
            pltpu.VMEM((table_rows, width), bf16),
            pltpu.VMEM((rows, width), f32),
            pltpu.VMEM((rows, width), f32),
            pltpu.VMEM((table_rows, width), bf16),
            pltpu.VMEM((groups, rows, width), i16),
            pltpu.VMEM((groups, 16, rows), f32),
            pltpu.VMEM((STOPS, rows, width), i16),
            pltpu.VMEM((STOPS, 8, rows), f32),
            pltpu.VMEM((groups, 8, rows), f32),
            pltpu.VMEM((groups, 8, rows), f32),
            pltpu.VMEM((groups, rows, width), bf16),
            pltpu.VMEM((groups, rows, width), bf16),
            pltpu.VMEM((8, rows), f32),
            pltpu.VMEM((groups, 8, rows), f32),
            pltpu.VMEM((STOPS, rows, width), bf16),
            pltpu.VMEM((STOPS, rows, width), bf16),
            pltpu.VMEM((8, rows), f32),
            pltpu.VMEM((loops, 8, rows), f32),
            pltpu.VMEM((groups, table_rows, rows), f32),
            pltpu.VMEM((groups, table_rows, rows), f32),
            pltpu.VMEM((STOPS * rows, rows), f32),
            pltpu.VMEM(((STOPS - 1) * rows, width), bf16),
            pltpu.VMEM(((STOPS - 1) * rows, width), bf16),
            pltpu.VMEM((STOPS - 1, rows, width), f32),
            pltpu.VMEM((groups * rows, width), bf16),
            pltpu.VMEM((groups * rows, width), bf16),
            pltpu.VMEM((table_rows, groups * rows), bf16),
            pltpu.SemaphoreType.DMA((8, max(groups, STOPS) + 1)),
            pltpu.SemaphoreType.DMA((8, max(groups, STOPS) + 1)),
            pltpu.SemaphoreType.DMA((loops,)),
            pltpu.SemaphoreType.DMA((loops,)),
            pltpu.SemaphoreType.DMA((3,)),
            pltpu.SemaphoreType.DMA((3,)),
        ],
        compiler_params=pltpu.CompilerParams(
            collective_id=0, has_side_effects=True, vmem_limit_bytes=60 * 1024 * 1024
        ),
    )(queries, passages, hard_table, index)
    done = pl.pallas_call(
        hand_over,
        out_shape=tuple(jax.ShapeDtypeStruct(x.shape, x.dtype) for x in out[1:]),
        in_specs=[anywhere] * 3,
        out_specs=(anywhere,) * 3,
        scratch_shapes=[pltpu.VMEM(x.shape, x.dtype) for x in out[1:]]
        + [pltpu.SemaphoreType.DMA((12,)), pltpu.SemaphoreType.DMA((12,))],
        compiler_params=pltpu.CompilerParams(vmem_limit_bytes=60 * 1024 * 1024),
    )(*out[1:])
    return (out[0].reshape(()),) + tuple(done)


def solution(mesh):
    rows = P(("blk", "grp"), None)
    return jax.shard_map(
        functools.partial(local, mesh.shape["blk"], mesh.shape["grp"]),
        mesh=mesh,
        in_specs=(rows, rows, rows, rows),
        out_specs=(P(), rows, rows, rows),
        check_vma=False,
    )
```

profile of v0, /device:TPU:1, one launch (start us, length us, event | category | flops | bytes accessed | tf_op | source)
XLA Modules:
  0.0 59.0 jit_solution(1757438218261626211)
XLA Ops:
  0.6 54.0 %shard_map.75 = (f32[1,1]{1,0:T(1,128)}, f32[128,1024]{1,0:T(8,128)}, f32[128,1024]{1,0:T(8,128)}, bf16[768,1024]{1,0:T(8,128)(2,1)}) custom-call(f32[128,1024]{1,0:T(8,128)} %q_hbm.1, f32[128,1024]{1,0:T(8,128)} %p_hbm.1, bf16[768,1024]{1,0:T(8,128)(2,1)} %t_hbm.1, s32[8,128]{1,0:T(8,128)} %bitcast.2), custom_call_target="tpu_custom_call" | custom-call | tf_op jit(solution)/shard_map/pallas_call | solution.py:423
  54.6 2.7 %shard_map.76 = (f32[128,1024]{1,0:T(8,128)}, f32[128,1024]{1,0:T(8,128)}, bf16[768,1024]{1,0:T(8,128)(2,1)}) custom-call(f32[128,1024]{1,0:T(8,128)} %get-tuple-element.12.a_ref, f32[128,1024]{1,0:T(8,128)} %get-tuple-element.13.b_ref, bf16[768,1024]{1,0:T(8,128)(2,1)} %get-tuple-element.14.c_ref), custom_call_target="tpu_custom_call" | custom-call | tf_op jit(solution)/shard_map/pallas_call | solution.py:474
where the time goes:
time: 59.2 us; the launch traced here: 59 us
  Pallas kernels  56.6 us (96%)
  between operations  2.33 us (4%)
    pallas_call x1, Pallas kernels, local(): pl.pallas_call(functools.partial(kernel, loops, groups), out_shape=(jax.S...  54 us
    pallas_call x1, Pallas kernels, local(): pl.pallas_call(hand_over, out_shape=tuple((jax.ShapeDtypeStruct(x.shape,...  2.68 us

commit v1 on v0

--- a/solution.py
+++ b/solution.py
@@ -14,7 +14,7 @@
 MESH = pl.DeviceIdType.MESH
 HIGHEST = lax.Precision.HIGHEST
 
-QUERY, QUERY_META, PASSAGE, PASSAGE_META, STATS, PARTIAL, LSE, GRAD = range(8)
+QUERY, QUERY_META, PASSAGE, PASSAGE_META, STATS, PARTIAL, LSE, GRAD, MERGE, MERGE_META = range(10)
 
 
 def as_column(row, count):
@@ -57,7 +57,7 @@
     loops, groups,
     q_hbm, p_hbm, t_hbm, idx_ref,
     loss_ref, qg_out, pg_out, tg_out,
-    q_ref, p_ref, t_ref, qg_ref, pg_ref, tg_ref, q16, qmeta, p16, pmeta, st_send, st_recv, a_send, a_recv, lse_send, lse_recv,
+    q_ref, p_ref, t_ref, qg_ref, pg_ref, tg_ref, q16, qmeta, p16, pmeta, st_send, st_recv, a_send, a_recv, af, m_stat, m_recv, lse_send, lse_recv,
     g_send, g_recv, l_send, l_recv, sh, ch, sw, phi, plo, gf, qhi, qlo, whi,
     send_sem, recv_sem, lsend_sem, lrecv_sem, load_sem, save_sem,
 ):
@@ -104,14 +104,11 @@
     def arrived(kind, slot, ref):
         copy(kind, 0, ref, ref, (b, lax.rem(g + 1, groups)), slot).wait_recv()
 
-    near = jnp.minimum(g, groups - 1 - g)
-    right_longer = (g < groups - 1 - g).astype(jnp.int32)
-    others = [None]
-    for i in range(groups - 1):
-        both = (i < 2 * near).astype(jnp.int32)
-        distance = both * (i // 2 + 1) + (1 - both) * (i - near + 1)
-        right = both * (i % 2) + (1 - both) * right_longer
-        others.append(g + distance * (2 * right - 1))
+    assert groups == 4
+    half = g // 2
+    inner = lax.rem(g, 2) == 1 - half
+    near = inner.astype(jnp.int32)
+    others = [None, g + 1 - 2 * lax.rem(g, 2), 2 - half, 3 - 3 * half]
 
     own_right = copy(QUERY, 0, q16.at[g], q16.at[g], (b, jnp.minimum(g + 1, groups - 1)), g)
     own_left = copy(QUERY, groups, q16.at[g], q16.at[g], (b, jnp.maximum(g - 1, 0)), g)
@@ -188,9 +185,42 @@
         st_send[j, 1:2, :] = jnp.sum(part, axis=0, keepdims=True)
         if j > 0:
             go(STATS, j, st_send.at[j], st_recv.at[g], (b, src), g)
-        a_send[j] = mm(part.T.astype(jnp.bfloat16), table).astype(jnp.bfloat16)
-        if j > 0:
-            go(PARTIAL, j, a_send.at[j], a_recv.at[g], (b, src), g)
+        partial = mm(part.T.astype(jnp.bfloat16), table)
+        if j == 0:
+            af[0] = partial
+        elif j == 1:
+            a_send[j] = partial.astype(jnp.bfloat16)
+            go(PARTIAL, j, a_send.at[j], a_recv.at[0], (b, src), 0)
+        else:
+            af[j - 1] = partial
+
+            @pl.when(jnp.logical_not(inner))
+            def _():
+                a_send[j] = partial.astype(jnp.bfloat16)
+                merge_stats(j).start()
+                merge_block(j).start()
+
+    def merge_stats(j):
+        return copy(MERGE_META, j, st_send.at[j], m_stat.at[j - 2], (b, others[1]))
+
+    def merge_block(j):
+        return copy(MERGE, j, a_send.at[j], m_recv.at[j - 2], (b, others[1]))
+
+    def joined_block(j):
+        return copy(PARTIAL, j, a_send.at[j], a_recv.at[1], (b, others[j]), 1)
+
+    def join(j):
+        @pl.when(inner)
+        def _():
+            merge_stats(j).wait_recv()
+            merge_block(j).wait_recv()
+            here, there = st_send[j, 0:1, :], m_stat[j - 2, 0:1, :]
+            most = jnp.maximum(here, there)
+            a_send[j] = (
+                af[j - 1] * as_column(jnp.exp(here - most), rows)
+                + m_recv[j - 2].astype(jnp.float32) * as_column(jnp.exp(there - most), rows)
+            ).astype(jnp.bfloat16)
+            joined_block(j).start()
 
     def window_part(s):
         if s == 0:
@@ -241,13 +271,21 @@
         copies[PASSAGE, s].wait_recv()
     go(PASSAGE, 2, p16.at[1 + 2 * odd], p16.at[2], (partner, g))
     window_next(1)
-    for j in range(2, groups):
-        if j > 2:
-            receive(j)
-        if j == groups - 1:
-            for s in range(2, STOPS):
-                window_next(s)
-        hard_part(j)
+
+    @pl.when(near > 0)
+    def _():
+        receive(3)
+
+    hard_part(2)
+
+    @pl.when(near == 0)
+    def _():
+        receive(3)
+
+    for s in range(2, STOPS):
+        window_next(s)
+    hard_part(3)
+    join(2)
 
     window = sw[...]
     tops = [jnp.max(window, axis=0, keepdims=True), st_send[0, 0:1, :]]
@@ -282,6 +320,7 @@
         sw[0:rows, :], query, precision=HIGHEST, preferred_element_type=jnp.float32
     )
 
+    join(3)
     group_loss = lse_send[1:2, :]
     whi[:, 0:rows] = (
         ch[0] * jnp.exp(jnp.minimum(sh[0] - lse, 0.0)) * (qmeta[g, 8:9, :] * SCALE)
@@ -353,10 +392,14 @@
         + (mm(whi_, phi[...]) + mm(wlo_, phi[...]) + mm(whi_, plo[...]))
     )
 
-    parts = a_send[0].astype(jnp.float32) * as_column(jnp.exp(tops[1] - lse), rows)
-    for j in range(1, groups):
-        arrived(PARTIAL, others[j], a_recv.at[others[j]])
-        parts = parts + a_recv[others[j]].astype(jnp.float32) * as_column(jnp.exp(tops[j + 1] - lse), rows)
+    arrived(PARTIAL, 0, a_recv.at[0])
+    arrived(PARTIAL, 1, a_recv.at[1])
+    parts = (
+        af[0] * as_column(jnp.exp(tops[1] - lse), rows)
+        + a_recv[0].astype(jnp.float32) * as_column(jnp.exp(tops[2] - lse), rows)
+        + a_recv[1].astype(jnp.float32)
+        * as_column(jnp.exp(jnp.maximum(tops[3], tops[4]) - lse), rows)
+    )
     qg_ref[...] = (qg_ref[...] + parts) * SCALE
     saves[1].start()
     sums = pg_ref[...]
@@ -374,6 +417,17 @@
     loss_ref[0, 0] = jnp.sum(l_recv[:, 0:1, 0:1]) / (rows * loops * groups)
     for each in copies.values():
         each.wait_send()
+
+    for j in range(2, groups):
+
+        @pl.when(inner)
+        def _():
+            joined_block(j).wait_send()
+
+        @pl.when(jnp.logical_not(inner))
+        def _():
+            merge_stats(j).wait_send()
+            merge_block(j).wait_send()
 
     @pl.when(g < groups - 1)
     def _():
@@ -444,7 +498,10 @@
             pltpu.VMEM((groups, 8, rows), f32),
             pltpu.VMEM((groups, 8, rows), f32),
             pltpu.VMEM((groups, rows, width), bf16),
-            pltpu.VMEM((groups, rows, width), bf16),
+            pltpu.VMEM((2, rows, width), bf16),
+            pltpu.VMEM((groups - 1, rows, width), f32),
+            pltpu.VMEM((2, 8, rows), f32),
+            pltpu.VMEM((2, rows, width), bf16),
             pltpu.VMEM((8, rows), f32),
             pltpu.VMEM((groups, 8, rows), f32),
             pltpu.VMEM((STOPS, rows, width), bf16),
@@ -460,8 +517,8 @@
             pltpu.VMEM((groups * rows, width), bf16),
             pltpu.VMEM((groups * rows, width), bf16),
             pltpu.VMEM((table_rows, groups * rows), bf16),
-            pltpu.SemaphoreType.DMA((8, max(groups, STOPS) + 1)),
-            pltpu.SemaphoreType.DMA((8, max(groups, STOPS) + 1)),
+            pltpu.SemaphoreType.DMA((10, max(groups, STOPS) + 1)),
+            pltpu.SemaphoreType.DMA((10, max(groups, STOPS) + 1)),
             pltpu.SemaphoreType.DMA((loops,)),
             pltpu.SemaphoreType.DMA((loops,)),
             pltpu.SemaphoreType.DMA((3,)),

time: 59.2 us -> 57.3 us (0.968)
  the two profiles are of different devices: /device:TPU:1 before, /device:TPU:0 now
where the time goes in v1:
time: 57.3 us; the launch traced here: 57.1 us
  Pallas kernels  54.8 us (96%)
  between operations  2.33 us (4%)
    pallas_call x1, Pallas kernels, local(): pl.pallas_call(functools.partial(kernel, loops, groups), out_shape=(jax.S...  52.1 us
    pallas_call x1, Pallas kernels, local(): pl.pallas_call(hand_over, out_shape=tuple((jax.ShapeDtypeStruct(x.shape,...  2.68 us

profile of v1, /device:TPU:0, one launch (start us, length us, event | category | flops | bytes accessed | tf_op | source)
XLA Modules:
  0.0 57.1 jit_solution(1634031749114399857)
XLA Ops:
  0.6 52.1 %shard_map.75 = (f32[1,1]{1,0:T(1,128)}, f32[128,1024]{1,0:T(8,128)}, f32[128,1024]{1,0:T(8,128)}, bf16[768,1024]{1,0:T(8,128)(2,1)}) custom-call(f32[128,1024]{1,0:T(8,128)} %q_hbm.1, f32[128,1024]{1,0:T(8,128)} %p_hbm.1, bf16[768,1024]{1,0:T(8,128)(2,1)} %t_hbm.1, s32[8,128]{1,0:T(8,128)} %bitcast.2), custom_call_target="tpu_custom_call" | custom-call | tf_op jit(solution)/shard_map/pallas_call | solution.py:477
  52.7 2.7 %shard_map.76 = (f32[128,1024]{1,0:T(8,128)}, f32[128,1024]{1,0:T(8,128)}, bf16[768,1024]{1,0:T(8,128)(2,1)}) custom-call(f32[128,1024]{1,0:T(8,128)} %get-tuple-element.12.a_ref, f32[128,1024]{1,0:T(8,128)} %get-tuple-element.13.b_ref, bf16[768,1024]{1,0:T(8,128)(2,1)} %get-tuple-element.14.c_ref), custom_call_target="tpu_custom_call" | custom-call | tf_op jit(solution)/shard_map/pallas_call | solution.py:531

commit v2 on v1

--- a/solution.py
+++ b/solution.py
@@ -58,7 +58,7 @@
     q_hbm, p_hbm, t_hbm, idx_ref,
     loss_ref, qg_out, pg_out, tg_out,
     q_ref, p_ref, t_ref, qg_ref, pg_ref, tg_ref, q16, qmeta, p16, pmeta, st_send, st_recv, a_send, a_recv, af, m_stat, m_recv, lse_send, lse_recv,
-    g_send, g_recv, l_send, l_recv, sh, ch, sw, phi, plo, gf, qhi, qlo, whi,
+    g_send, g_recv, l_send, l_recv, ch, sw, phi, plo, gf, qhi, qlo, whi, w_top,
     send_sem, recv_sem, lsend_sem, lrecv_sem, load_sem, save_sem,
 ):
     b = lax.axis_index("blk")
@@ -180,7 +180,7 @@
         named = ch[j]
         top = jnp.max(jnp.where(named > 0.0, scores, LOW), axis=0, keepdims=True)
         part = named * jnp.exp(jnp.minimum(scores - top, 0.0))
-        sh[j] = scores
+        ch[j] = part
         st_send[j, 0:1, :] = top
         st_send[j, 1:2, :] = jnp.sum(part, axis=0, keepdims=True)
         if j > 0:
@@ -237,6 +237,23 @@
             scores * as_column(pmeta[s, 0:1, :], rows) * (qmeta[g, 8:9, :] * SCALE)
         )
 
+    def window_grad():
+        top = jnp.max(sw[...], axis=0, keepdims=True)
+        sw[...] = jnp.exp(sw[...] - top)
+        w_top[...] = jnp.broadcast_to(top, (8, rows))
+        high, low = two_terms(
+            jnp.concatenate(
+                [
+                    sw[s * rows:(s + 1) * rows, :] * as_column(pmeta[s, 0:1, :], rows)
+                    for s in range(1, STOPS)
+                ],
+                axis=0,
+            ).T
+        )
+        qg_ref[...] = jnp.dot(
+            sw[0:rows, :].T, p_ref[...], precision=HIGHEST, preferred_element_type=jnp.float32
+        ) + (mm(high, phi[...]) + mm(low, phi[...]) + mm(high, plo[...]))
+
     st_send[...] = jnp.zeros_like(st_send)
     count(0)
     hard_part(0)
@@ -278,22 +295,28 @@
 
     hard_part(2)
 
-    @pl.when(near == 0)
-    def _():
-        receive(3)
-
     for s in range(2, STOPS):
         window_next(s)
+
+    @pl.when(near == 0)
+    def _():
+        window_grad()
+        receive(3)
+
     hard_part(3)
+
+    @pl.when(near > 0)
+    def _():
+        window_grad()
+
     join(2)
 
-    window = sw[...]
-    tops = [jnp.max(window, axis=0, keepdims=True), st_send[0, 0:1, :]]
+    tops = [w_top[0:1, :], st_send[0, 0:1, :]]
     for j in range(1, groups):
         arrived(STATS, others[j], st_recv.at[others[j]])
         tops.append(st_recv[others[j], 0:1, :])
     top = functools.reduce(jnp.maximum, tops)
-    total = jnp.sum(jnp.exp(window - top), axis=0, keepdims=True)
+    total = jnp.sum(sw[...], axis=0, keepdims=True) * jnp.exp(tops[0] - top)
     total = total + st_send[0, 1:2, :] * jnp.exp(tops[1] - top)
     for j in range(1, groups):
         total = total + st_recv[others[j], 1:2, :] * jnp.exp(tops[j + 1] - top)
@@ -303,7 +326,7 @@
     for j in range(1, groups):
         go(LSE, j, lse_send, lse_recv.at[g], (b, others[j]), g)
 
-    sw[...] = jnp.exp(window - lse)
+    sw[...] = sw[...] * jnp.exp(tops[0] - lse)
     whi_, wlo_ = two_terms(sw[rows:, :] * qmeta[g, 8:9, :])
     terms = mm(
         jnp.concatenate([whi_, whi_], axis=1),
@@ -320,18 +343,21 @@
         sw[0:rows, :], query, precision=HIGHEST, preferred_element_type=jnp.float32
     )
 
+    copies[GRAD, 0].wait_recv()
+    g_send[STOPS - 1] = (gf[joined - 1] + g_recv[0].astype(jnp.float32)).astype(jnp.bfloat16)
+    go(GRAD, 2, g_send.at[STOPS - 1], g_recv.at[2], (lax.rem(b + loops - joined, loops), g))
     join(3)
     group_loss = lse_send[1:2, :]
     whi[:, 0:rows] = (
-        ch[0] * jnp.exp(jnp.minimum(sh[0] - lse, 0.0)) * (qmeta[g, 8:9, :] * SCALE)
+        ch[0] * (jnp.exp(tops[1] - lse) * (qmeta[g, 8:9, :] * SCALE))
     ).astype(jnp.bfloat16)
     for j in range(1, groups):
-        arrived(LSE, others[j], lse_recv.at[others[j]])
-        group_loss = group_loss + lse_recv[others[j], 1:2, :]
-        whi[:, j * rows:(j + 1) * rows] = jnp.where(
-            ch[j] > 0.0,
-            ch[j] * jnp.exp(jnp.minimum(sh[j] - lse_recv[others[j], 0:1, :], 0.0)) * (qmeta[others[j], 8:9, :] * SCALE),
-            0.0,
+        src = others[j]
+        arrived(LSE, src, lse_recv.at[src])
+        group_loss = group_loss + lse_recv[src, 1:2, :]
+        factor = jnp.exp(jnp.minimum(st_send[j, 0:1, :] - lse_recv[src, 0:1, :], 0.0))
+        whi[:, j * rows:(j + 1) * rows] = (
+            ch[j] * (factor * (qmeta[src, 8:9, :] * SCALE))
         ).astype(jnp.bfloat16)
 
     l_send[...] = jnp.broadcast_to(group_loss, (8, rows))
@@ -353,10 +379,6 @@
 
     lax.fori_loop(1, loops, loss_start, 0)
 
-    copies[GRAD, 0].wait_recv()
-    g_send[STOPS - 1] = (gf[joined - 1] + g_recv[0].astype(jnp.float32)).astype(jnp.bfloat16)
-    go(GRAD, 2, g_send.at[STOPS - 1], g_recv.at[2], (lax.rem(b + loops - joined, loops), g))
-
     tile = 256
 
     def table_tile(step, carry):
@@ -375,30 +397,16 @@
     ]
     saves[0].start()
 
-    whi_, wlo_ = two_terms(
-        jnp.concatenate(
-            [
-                sw[s * rows:(s + 1) * rows, :] * as_column(pmeta[s, 0:1, :], rows)
-                for s in range(1, STOPS)
-            ],
-            axis=0,
-        ).T
+    qg_ref[...] = (
+        qg_ref[...] * as_column(jnp.exp(tops[0] - lse), rows)
+        + af[0] * as_column(jnp.exp(tops[1] - lse), rows)
+        - p_ref[...]
     )
-    qg_ref[...] = (
-        jnp.dot(
-            sw[0:rows, :].T, p_ref[...], precision=HIGHEST, preferred_element_type=jnp.float32
-        )
-        - p_ref[...]
-        + (mm(whi_, phi[...]) + mm(wlo_, phi[...]) + mm(whi_, plo[...]))
-    )
-
     arrived(PARTIAL, 0, a_recv.at[0])
+    parts = a_recv[0].astype(jnp.float32) * as_column(jnp.exp(tops[2] - lse), rows)
     arrived(PARTIAL, 1, a_recv.at[1])
-    parts = (
-        af[0] * as_column(jnp.exp(tops[1] - lse), rows)
-        + a_recv[0].astype(jnp.float32) * as_column(jnp.exp(tops[2] - lse), rows)
-        + a_recv[1].astype(jnp.float32)
-        * as_column(jnp.exp(jnp.maximum(tops[3], tops[4]) - lse), rows)
+    parts = parts + a_recv[1].astype(jnp.float32) * as_column(
+        jnp.exp(jnp.maximum(tops[3], tops[4]) - lse), rows
     )
     qg_ref[...] = (qg_ref[...] + parts) * SCALE
     saves[1].start()
@@ -509,7 +517,6 @@
             pltpu.VMEM((8, rows), f32),
             pltpu.VMEM((loops, 8, rows), f32),
             pltpu.VMEM((groups, table_rows, rows), f32),
-            pltpu.VMEM((groups, table_rows, rows), f32),
             pltpu.VMEM((STOPS * rows, rows), f32),
             pltpu.VMEM(((STOPS - 1) * rows, width), bf16),
             pltpu.VMEM(((STOPS - 1) * rows, width), bf16),
@@ -517,6 +524,7 @@
             pltpu.VMEM((groups * rows, width), bf16),
             pltpu.VMEM((groups * rows, width), bf16),
             pltpu.VMEM((table_rows, groups * rows), bf16),
+            pltpu.VMEM((8, rows), f32),
             pltpu.SemaphoreType.DMA((10, max(groups, STOPS) + 1)),
             pltpu.SemaphoreType.DMA((10, max(groups, STOPS) + 1)),
             pltpu.SemaphoreType.DMA((loops,)),

time: 57.3 us -> 56.3 us (0.983)
  Pallas kernels: 54.8 us -> 53.7 us
    pallas_call x1, Pallas kernels: 52.1 us -> 51.1 us  [local(): pl.pallas_call(functools.partial(kernel, loops, groups), out_shape=(jax.S...]
where the time goes in v2:
time: 56.3 us; the launch traced here: 56.1 us
  Pallas kernels  53.7 us (95%)
  between operations  2.33 us (4%)
    pallas_call x1, Pallas kernels, local(): pl.pallas_call(functools.partial(kernel, loops, groups), out_shape=(jax.S...  51.1 us
    pallas_call x1, Pallas kernels, local(): pl.pallas_call(hand_over, out_shape=tuple((jax.ShapeDtypeStruct(x.shape,...  2.68 us

profile of v2, /device:TPU:0, one launch (start us, length us, event | category | flops | bytes accessed | tf_op | source)
XLA Modules:
  0.0 56.1 jit_solution(15545354109898031853)
XLA Ops:
  0.6 51.1 %shard_map.75 = (f32[1,1]{1,0:T(1,128)}, f32[128,1024]{1,0:T(8,128)}, f32[128,1024]{1,0:T(8,128)}, bf16[768,1024]{1,0:T(8,128)(2,1)}) custom-call(f32[128,1024]{1,0:T(8,128)} %q_hbm.1, f32[128,1024]{1,0:T(8,128)} %p_hbm.1, bf16[768,1024]{1,0:T(8,128)(2,1)} %t_hbm.1, s32[8,128]{1,0:T(8,128)} %bitcast.2), custom_call_target="tpu_custom_call" | custom-call | tf_op jit(solution)/shard_map/pallas_call | solution.py:485
  51.7 2.7 %shard_map.76 = (f32[128,1024]{1,0:T(8,128)}, f32[128,1024]{1,0:T(8,128)}, bf16[768,1024]{1,0:T(8,128)(2,1)}) custom-call(f32[128,1024]{1,0:T(8,128)} %get-tuple-element.12.a_ref, f32[128,1024]{1,0:T(8,128)} %get-tuple-element.13.b_ref, bf16[768,1024]{1,0:T(8,128)(2,1)} %get-tuple-element.14.c_ref), custom_call_target="tpu_custom_call" | custom-call | tf_op jit(solution)/shard_map/pallas_call | solution.py:539

commit v3 on v2

--- a/solution.py
+++ b/solution.py
@@ -346,7 +346,6 @@
     copies[GRAD, 0].wait_recv()
     g_send[STOPS - 1] = (gf[joined - 1] + g_recv[0].astype(jnp.float32)).astype(jnp.bfloat16)
     go(GRAD, 2, g_send.at[STOPS - 1], g_recv.at[2], (lax.rem(b + loops - joined, loops), g))
-    join(3)
     group_loss = lse_send[1:2, :]
     whi[:, 0:rows] = (
         ch[0] * (jnp.exp(tops[1] - lse) * (qmeta[g, 8:9, :] * SCALE))
@@ -378,6 +377,7 @@
         return carry
 
     lax.fori_loop(1, loops, loss_start, 0)
+    join(3)
 
     tile = 256
 

time: 56.3 us -> 56.6 us (level)
  no operation moved by 1% of the time
where the time goes in v3:
time: 56.6 us; the launch traced here: 56.4 us
  Pallas kernels  54.1 us (96%)
  between operations  2.33 us (4%)
    pallas_call x1, Pallas kernels, local(): pl.pallas_call(functools.partial(kernel, loops, groups), out_shape=(jax.S...  51.4 us
    pallas_call x1, Pallas kernels, local(): pl.pallas_call(hand_over, out_shape=tuple((jax.ShapeDtypeStruct(x.shape,...  2.68 us

profile of v3, /device:TPU:0, one launch (start us, length us, event | category | flops | bytes accessed | tf_op | source)
XLA Modules:
  0.0 56.4 jit_solution(9581337823234179404)
XLA Ops:
  0.6 51.4 %shard_map.75 = (f32[1,1]{1,0:T(1,128)}, f32[128,1024]{1,0:T(8,128)}, f32[128,1024]{1,0:T(8,128)}, bf16[768,1024]{1,0:T(8,128)(2,1)}) custom-call(f32[128,1024]{1,0:T(8,128)} %q_hbm.1, f32[128,1024]{1,0:T(8,128)} %p_hbm.1, bf16[768,1024]{1,0:T(8,128)(2,1)} %t_hbm.1, s32[8,128]{1,0:T(8,128)} %bitcast.2), custom_call_target="tpu_custom_call" | custom-call | tf_op jit(solution)/shard_map/pallas_call | solution.py:485
  52.0 2.7 %shard_map.76 = (f32[128,1024]{1,0:T(8,128)}, f32[128,1024]{1,0:T(8,128)}, bf16[768,1024]{1,0:T(8,128)(2,1)}) custom-call(f32[128,1024]{1,0:T(8,128)} %get-tuple-element.12.a_ref, f32[128,1024]{1,0:T(8,128)} %get-tuple-element.13.b_ref, bf16[768,1024]{1,0:T(8,128)(2,1)} %get-tuple-element.14.c_ref), custom_call_target="tpu_custom_call" | custom-call | tf_op jit(solution)/shard_map/pallas_call | solution.py:539
